TPU v7x, 32 devices: a whole 2x2x4 slice. The times are simulated.
32 devices in a mesh: mem: 2 (over core), lat: 16 (over z, y, x).
Axes of the slice: x: 2, y: 2, z: 4, core: 2. Of those that a mesh axis runs over, the one named last changes fastest.
Arguments:
- members: bfloat16 [8, 4, 16, 128, 1024], P('mem', None, None, 'lat'), may hold values from -6 to 6
- increment: float32 [4, 16, 128, 1024], P(None, 'mem', 'lat'), may hold values from -6 to 6
- vertical: float32 [16, 16], replicated, may hold values from -1.5 to 1.5
- lat_taps: float32 [9], replicated, may hold values from 0.2 to 0.6
- lon_taps: float32 [9], replicated, may hold values from 0.2 to 0.6
Outputs:
- product: float32 [4, 16, 128, 1024], P(None, 'mem', 'lat')
All inputs are finite; a program needn't handle non-finite values.
Results may differ from a plain program's by a relative error of at most 0.0003.
Values sent between devices are 32-bit elements; how exact they have to be, the bound alone decides.
A program may use at most 64 MiB of HBM per device.

v0:
```python
import jax
import jax.numpy as jnp
from jax import lax
from jax.sharding import PartitionSpec as P


def extended(block, sides, width):
    for axis, dim in sides:
        count = lax.axis_size(axis)
        forward = [(i, i + 1) for i in range(count - 1)]
        backward = [(target, source) for source, target in forward]
        low = lax.ppermute(
            lax.slice_in_dim(block, block.shape[dim] - width, None, axis=dim), axis, forward
        )
        high = lax.ppermute(lax.slice_in_dim(block, 0, width, axis=dim), axis, backward)
        block = jnp.concatenate([low, block, high], axis=dim)
    return block


def lon_adjoint(source, kernel):
    summed = jnp.zeros(source.shape, jnp.float32)
    for offset in range(9):
        summed = summed + kernel[offset] * jnp.roll(source, offset - 4, axis=-1)
    return summed


def lon_forward(source, kernel):
    summed = jnp.zeros(source.shape, jnp.float32)
    for offset in range(9):
        summed = summed + kernel[offset] * jnp.roll(source, 4 - offset, axis=-1)
    return summed


def lat_adjoint(padded, kernel):
    row_count = padded.shape[-2] - 8
    summed = kernel[0] * padded[..., 8 : 8 + row_count, :]
    for offset in range(1, 9):
        summed = summed + kernel[offset] * padded[..., 8 - offset : 8 - offset + row_count, :]
    return summed


def lat_forward(padded, kernel):
    row_count = padded.shape[-2] - 8
    summed = kernel[0] * padded[..., 0:row_count, :]
    for offset in range(1, 9):
        summed = summed + kernel[offset] * padded[..., offset : offset + row_count, :]
    return summed


def per_device(members, increment, vertical, lat_taps, lon_taps):
    increment_all = lax.all_gather(increment, "mem", axis=1, tiled=True)
    values = members.astype(jnp.float32)
    weighted = jnp.sum(values * increment_all[None], axis=1)
    weighted = lon_adjoint(weighted, lon_taps)
    weighted = jnp.einsum("kl,mkij->mlij", vertical, weighted, precision=lax.Precision.HIGHEST)
    padded = extended(weighted, (("lat", 2),), 4)
    adjoint_field = lat_adjoint(padded, lat_taps)
    padded = extended(adjoint_field, (("lat", 2),), 4)
    spread = lat_forward(padded, lat_taps)
    spread = lon_forward(spread, lon_taps)
    spread = jnp.einsum("lk,mkij->mlij", vertical, spread, precision=lax.Precision.HIGHEST)
    member_count = members.shape[0] * lax.axis_size("mem")
    member_terms = jnp.sum(values * spread[:, None], axis=0) / jnp.float32(member_count - 1)
    return lax.psum_scatter(member_terms, "mem", scatter_dimension=1, tiled=True)


def solution(mesh):
    in_specs = (P("mem", None, None, "lat", None), P(None, "mem", "lat", None), P(), P(), P())
    out_specs = P(None, "mem", "lat", None)
    return jax.shard_map(
        per_device, mesh=mesh, in_specs=in_specs, out_specs=out_specs, check_vma=False
    )
```

profile of v0, /device:TPU:7, one launch (start us, length us, event | category | flops | bytes accessed | tf_op | source)
XLA Modules:
  0.0 211.1 jit_solution(6759201833913844329)
XLA Ops:
  6.5 0.7 all-gather.2.cloned.1.call-update
  7.3 1.7 fusion.148
  9.0 12.5 %all-gather.2.cloned.1.call-done = f32[4,16,8,1024]{3,2,1,0:T(8,128)} async-done(((f32[4,8,8,1024]{3,2,1,0:T(8,128)}), f32[4,16,8,1024]{3,2,1,0:T(8,128)}) %all-gather.2.cloned.1.call-update) | async-done | bytes 2097168 | tf_op jit(solution)/shard_map/all_gather | solution.py:51
  21.4 4.3 %fusion = f32[4,16,8,1024]{3,2,1,0:T(8,128)S(1)} fusion(bf16[4,4,16,8,1024]{4,3,2,1,0:T(8,128)(2,1)} %param.5, f32[4,16,8,1024]{3,2,1,0:T(8,128)} %all-gather.2.cloned.1.call-done), kind=kLoop, calls=%fused_computation.2 | loop fusion | flops 5767168 | bytes 8388608 | tf_op jit(solution)/shard_map/reduce_sum | solution.py:53
  25.7 0.8 fusion.140
  26.5 0.8 fusion.142
  27.2 0.8 fusion.144
  28.0 0.8 fusion.146
  28.9 0.2 fusion.139
  29.0 0.1 fusion.141
  29.2 0.1 fusion.143
  29.3 0.1 fusion.145
  29.5 1.2 copy.40
  30.7 1.2 copy.42
  31.9 1.2 copy.44
  33.1 1.2 copy.46
  34.4 1.2 copy.47
  35.6 1.4 copy.49
  37.0 1.2 copy.51
  38.2 1.2 copy.53
  39.9 12.5 %fusion.103 = f32[4,16,8,1024]{3,1,2,0:T(8,128)S(1)} fusion(f32[4,16,8,4]{3,1,2,0:T(8,128)S(1)} %copy.39, f32[4,16,8,1020]{3,1,2,0:T(8,128)S(1)} %copy.40, f32[4,16,8,3]{3,1,2,0:T(8,128)S(1)} %copy.41, f32[4,16,8,1021]{3,1,2,0:T(8,128)S(1)} %copy.42, f32[4,16,8,2]{3,1,2,0:T(8,128)S(1)} %copy.43, f32[4,16,8,1022]{3,1,2,0:T(8,128)S(1)} %copy.44, ...), kind=kOutput, calls=%fused_computation.145 | convolution fusion | flops 113770496 | bytes 20972580 | tf_op jit(solution)/shard_map/kl,mkij->mlij/dot_general | solution.py:55
  52.6 2.2 %collective-permute-start = (f32[4,16,4,1024]{3,1,2,0:T(8,128)S(1)}, f32[4,16,4,1024]{3,1,2,0:T(8,128)S(1)}, u32[]{:S(2)}, u32[]{:S(2)}) collective-permute-start(f32[4,16,4,1024]{3,1,2,0:T(8,128)S(1)} %get-tuple-element.23), channel_id=1, source_target_pairs={{1,0},{2,1},{3,2},{4,3},{5,4},{6,5},{7,6},{8,7},{9,8},{10,9},{11,1... | collective-permute-start | bytes 3145736 | tf_op jit(solution)/shard_map/ppermute | solution.py:15
  54.8 4.9 %collective-permute-start.1 = (f32[4,16,4,1024]{3,1,2,0:T(8,128)S(1)}, f32[4,16,4,1024]{3,1,2,0:T(8,128)S(1)}, u32[]{:S(2)}, u32[]{:S(2)}) collective-permute-start(f32[4,16,4,1024]{3,1,2,0:T(8,128)S(1)} %get-tuple-element.24), channel_id=1, source_target_pairs={{0,1},{1,2},{2,3},{3,4},{4,5},{5,6},{6,7},{7,8},{8,9},{9,10},{10,1... | collective-permute-start | bytes 3145736 | tf_op jit(solution)/shard_map/ppermute | solution.py:12
  59.7 0.7 fusion.147
  60.4 20.5 %collective-permute-done = f32[4,16,4,1024]{3,1,2,0:T(8,128)S(1)} collective-permute-done((f32[4,16,4,1024]{3,1,2,0:T(8,128)S(1)}, f32[4,16,4,1024]{3,1,2,0:T(8,128)S(1)}, u32[]{:S(2)}, u32[]{:S(2)}) %collective-permute-start) | collective-permute-done | bytes 1048608 | tf_op jit(solution)/shard_map/ppermute | solution.py:15
  80.9 20.6 %collective-permute-done.1 = f32[4,16,4,1024]{3,1,2,0:T(8,128)S(1)} collective-permute-done((f32[4,16,4,1024]{3,1,2,0:T(8,128)S(1)}, f32[4,16,4,1024]{3,1,2,0:T(8,128)S(1)}, u32[]{:S(2)}, u32[]{:S(2)}) %collective-permute-start.1) | collective-permute-done | bytes 1048608 | tf_op jit(solution)/shard_map/ppermute | solution.py:12
  101.5 8.1 %fusion.25 = f32[4,16,8,1024]{3,1,2,0:T(8,128)S(1)} fusion(f32[4,16,8,1024]{3,1,2,0:T(8,128)S(1)} %fusion.103, f32[4,16,4,1024]{3,1,2,0:T(8,128)S(1)} %collective-permute-done.1, f32[4,16,4,1024]{3,1,2,0:T(8,128)S(1)} %collective-permute-done, f32[]{:T(128)} %bitcast.19, f32[]{:T(128)} %bitcast.18, f32[]{:T(128)} %bitcast.17, f32[]{:T(128)} %bitcast.16, ...), kind=kLoop, calls=%fused_computation.51 | loop fusion | flops 13107200 | bytes 6291492 | tf_op jit(solution)/shard_map/add | solution.py:38
  109.7 4.5 %collective-permute-start.2 = (f32[4,16,4,1024]{3,1,2,0:T(8,128)S(1)}, f32[4,16,4,1024]{3,1,2,0:T(8,128)S(1)}, u32[]{:S(2)}, u32[]{:S(2)}) collective-permute-start(f32[4,16,4,1024]{3,1,2,0:T(8,128)S(1)} %get-tuple-element.21), channel_id=1, source_target_pairs={{0,1},{1,2},{2,3},{3,4},{4,5},{5,6},{6,7},{7,8},{8,9},{9,10},{10,1... | collective-permute-start | bytes 3145736 | tf_op jit(solution)/shard_map/ppermute | solution.py:12
  114.2 2.1 %collective-permute-start.3 = (f32[4,16,4,1024]{3,1,2,0:T(8,128)S(1)}, f32[4,16,4,1024]{3,1,2,0:T(8,128)S(1)}, u32[]{:S(2)}, u32[]{:S(2)}) collective-permute-start(f32[4,16,4,1024]{3,1,2,0:T(8,128)S(1)} %get-tuple-element.22), channel_id=1, source_target_pairs={{1,0},{2,1},{3,2},{4,3},{5,4},{6,5},{7,6},{8,7},{9,8},{10,9},{11,1... | collective-permute-start | bytes 3145736 | tf_op jit(solution)/shard_map/ppermute | solution.py:15
  116.3 19.9 %collective-permute-done.2 = f32[4,16,4,1024]{3,1,2,0:T(8,128)S(1)} collective-permute-done((f32[4,16,4,1024]{3,1,2,0:T(8,128)S(1)}, f32[4,16,4,1024]{3,1,2,0:T(8,128)S(1)}, u32[]{:S(2)}, u32[]{:S(2)}) %collective-permute-start.2) | collective-permute-done | bytes 1048608 | tf_op jit(solution)/shard_map/ppermute | solution.py:12
  136.3 5.6 %collective-permute-done.3 = f32[4,16,4,1024]{3,1,2,0:T(8,128)S(1)} collective-permute-done((f32[4,16,4,1024]{3,1,2,0:T(8,128)S(1)}, f32[4,16,4,1024]{3,1,2,0:T(8,128)S(1)}, u32[]{:S(2)}, u32[]{:S(2)}) %collective-permute-start.3) | collective-permute-done | bytes 1048608 | tf_op jit(solution)/shard_map/ppermute | solution.py:15
  141.9 8.2 %fusion.5 = f32[4,16,8,1024]{3,1,2,0:T(8,128)S(1)} fusion(f32[4,16,8,1024]{3,1,2,0:T(8,128)S(1)} %fusion.25, f32[4,16,4,1024]{3,1,2,0:T(8,128)S(1)} %collective-permute-done.3, f32[4,16,4,1024]{3,1,2,0:T(8,128)S(1)} %collective-permute-done.2, f32[]{:T(128)} %bitcast.19, f32[]{:T(128)} %bitcast.18, f32[]{:T(128)} %bitcast.17, f32[]{:T(128)} %bitcast.16, ...), kind=kLoop, calls=%fused_computation.31 | loop fusion | flops 13107200 | bytes 6291492 | tf_op jit(solution)/shard_map/add | solution.py:46
  150.1 0.7 fusion.131
  150.9 0.8 fusion.133
  151.7 0.8 fusion.135
  152.6 0.8 fusion.129
  153.4 0.2 fusion.132
  153.9 0.1 fusion.130
  154.1 11.9 %fusion.100 = f32[4,16,8,1024]{3,1,2,0:T(8,128)S(1)} fusion(f32[4,16,8,1020]{3,1,2,0:T(8,128)S(1)} %get-tuple-element.6, f32[4,16,8,4]{3,1,2,0:T(8,128)S(1)} %get-tuple-element.8, f32[4,16,8,1021]{3,1,2,0:T(8,128)S(1)} %get-tuple-element.10, f32[4,16,8,3]{3,1,2,0:T(8,128)S(1)} %get-tuple-element.12, f32[4,16,8,1022]{3,1,2,0:T(8,128)S(1)} %get-tuple-element.14, ...), kind=kOutput, calls=%fused_computation.144 | convolution fusion | flops 113770496 | bytes 20972580 | tf_op jit(solution)/shard_map/lk,mkij->mlij/dot_general | solution.py:61
  165.9 1.2 copy.26
  167.2 1.0 copy-done.1
  168.1 1.1 fusion.1
  169.2 0.2 broadcast_multiply_fusion
  169.5 0.2 copy.30
  169.7 2.6 %copy.32 = f32[2,8,32,1024]{3,1,2,0:T(8,128)} copy(f32[2,8,32,1024]{3,2,1,0:T(8,128)S(1)} %bitcast.45) | data formatting | bytes 4194304
  172.3 29.0 %reduce-scatter.5.cloned.1.call-done = f32[8,32768]{1,0:T(8,128)} async-done(((f32[16,32768]{1,0:T(8,128)}), f32[8,32768]{1,0:T(8,128)}) %reduce-scatter.5.cloned.1.call-update) | async-done | bytes 1048592
  201.3 1.8 copy.55
  203.2 1.1 copy.31
  (20 shorter events, 1.0 us)
Async XLA Ops:
  6.5 33.4 %copy-start = (f32[16,16]{1,0:T(8,128)S(1)}, f32[16,16]{1,0:T(8,128)}, u32[]{:S(2)}) copy-start(f32[16,16]{1,0:T(8,128)} %param.7) | copy-start | bytes 3076
  6.5 14.9 %all-gather.2.cloned.1.call-start = ((), (), s32[]{:S(2)}) async-start(), calls=%async_computation.1 | async-start | bytes 3145728 | tf_op jit(solution)/shard_map/all_gather | solution.py:51
  7.3 194.1 %reduce-scatter.5.cloned.1.call-start = ((), (), s32[]{:S(2)}) async-start(), calls=%async_computation.2 | async-start | bytes 3145728
  52.4 7.3 %copy-start.2 = (f32[9]{0:T(128)S(1)}, f32[9]{0:T(128)}, u32[]{:S(2)}) copy-start(f32[9]{0:T(128)} %param.8) | copy-start | bytes 112
  52.6 28.3 %collective-permute-start = (f32[4,16,4,1024]{3,1,2,0:T(8,128)S(1)}, f32[4,16,4,1024]{3,1,2,0:T(8,128)S(1)}, u32[]{:S(2)}, u32[]{:S(2)}) collective-permute-start(f32[4,16,4,1024]{3,1,2,0:T(8,128)S(1)} %get-tuple-element.23), channel_id=1, source_target_pairs={{1,0},{2,1},{3,2},{4,3},{5,4},{6,5},{7,6},{8,7},{9,8},{10,9},{11,1... | collective-permute-start | bytes 3145736 | tf_op jit(solution)/shard_map/ppermute | solution.py:15
  54.8 46.7 %collective-permute-start.1 = (f32[4,16,4,1024]{3,1,2,0:T(8,128)S(1)}, f32[4,16,4,1024]{3,1,2,0:T(8,128)S(1)}, u32[]{:S(2)}, u32[]{:S(2)}) collective-permute-start(f32[4,16,4,1024]{3,1,2,0:T(8,128)S(1)} %get-tuple-element.24), channel_id=1, source_target_pairs={{0,1},{1,2},{2,3},{3,4},{4,5},{5,6},{6,7},{7,8},{8,9},{9,10},{10,1... | collective-permute-start | bytes 3145736 | tf_op jit(solution)/shard_map/ppermute | solution.py:12
  109.7 26.5 %collective-permute-start.2 = (f32[4,16,4,1024]{3,1,2,0:T(8,128)S(1)}, f32[4,16,4,1024]{3,1,2,0:T(8,128)S(1)}, u32[]{:S(2)}, u32[]{:S(2)}) collective-permute-start(f32[4,16,4,1024]{3,1,2,0:T(8,128)S(1)} %get-tuple-element.21), channel_id=1, source_target_pairs={{0,1},{1,2},{2,3},{3,4},{4,5},{5,6},{6,7},{7,8},{8,9},{9,10},{10,1... | collective-permute-start | bytes 3145736 | tf_op jit(solution)/shard_map/ppermute | solution.py:12
  114.2 27.7 %collective-permute-start.3 = (f32[4,16,4,1024]{3,1,2,0:T(8,128)S(1)}, f32[4,16,4,1024]{3,1,2,0:T(8,128)S(1)}, u32[]{:S(2)}, u32[]{:S(2)}) collective-permute-start(f32[4,16,4,1024]{3,1,2,0:T(8,128)S(1)} %get-tuple-element.22), channel_id=1, source_target_pairs={{1,0},{2,1},{3,2},{4,3},{5,4},{6,5},{7,6},{8,7},{9,8},{10,9},{11,1... | collective-permute-start | bytes 3145736 | tf_op jit(solution)/shard_map/ppermute | solution.py:15
  165.9 2.2 %copy-start.1 = (bf16[4,4,16,8,1024]{4,3,2,1,0:T(8,128)(2,1)S(1)}, bf16[4,4,16,8,1024]{4,3,2,1,0:T(8,128)(2,1)}, u32[]{:S(2)}) copy-start(bf16[4,4,16,8,1024]{4,3,2,1,0:T(8,128)(2,1)} %param.5) | copy-start | bytes 12582916
Sparse Core Ops, SparseCore 0:
  8.9 12.4 all-gather.1
  172.4 28.8 reduce-scatter.4
where the time goes:
time: 212 us; the launch traced here: 211 us
  waiting for transfers between devices  109 us (51%)
  local copies, waits for them, and re-layouts  28.4 us (13%)
  matrix products  24.4 us (12%)
  other arithmetic  21.9 us (10%)
  between operations  13.8 us (7%)
  starting transfers between devices  13.7 us (6%)
    ppermute x2, waiting for transfers between devices, extended(): lax.ppermute(lax.slice_in_dim(block, block.shape[dim] - width, None, axis...  40.5 us
    unnamed x3, waiting for transfers between devices  29.8 us
    ppermute x2, waiting for transfers between devices, extended(): lax.ppermute(lax.slice_in_dim(block, 0, width, axis=dim), axis, backward)  26.1 us
    unnamed x26, local copies, waits for them, and re-layouts  17 us
    dot_general x1, matrix products, per_device(): jnp.einsum('kl,mkij->mlij', vertical, weighted, precision=lax.Precision.H...  12.5 us
    all_gather x1, waiting for transfers between devices, per_device(): increment_all = lax.all_gather(increment, 'mem', axis=1, tiled=True)  12.5 us
    dot_general x1, matrix products, per_device(): jnp.einsum('lk,mkij->mlij', vertical, spread, precision=lax.Precision.HIG...  11.9 us
    ppermute x2, starting transfers between devices, extended(): lax.ppermute(lax.slice_in_dim(block, block.shape[dim] - width, None, axis...  9.35 us
  transfers between devices with their start and end apart: 6, of which 6 were waited for; matrix products, arithmetic and copies ran while one was open for 1% of the time, Pallas kernels for 0%

commit v1 on v0

v1 whole, which is shorter than its diff:
```python
import functools

import jax
import jax.numpy as jnp
from jax import lax
from jax.experimental import pallas as pl
from jax.experimental.pallas import tpu as pltpu
from jax.sharding import PartitionSpec as P

LANES = 128
PIECE = 16
HIGHEST = lax.Precision.HIGHEST
MESH = pl.DeviceIdType.MESH


def kernel(
    n_mem, n_lat, levels, members_ref, inc_ref, vert_ref, lat_ref, lon_ref, out_ref,
    mem_v, inc_v, own, buf, acc, part, mats,
    load_sem, inc_sem, inc_send, inc_recv, xs, xr, ys, yr, zs, zr, ps, pr,
):
    count, variables, rows, lon = mem_v.shape
    slab = rows // levels
    taps = lat_ref.shape[0]
    reach = taps // 2
    chunks = lon // LANES
    items = count * chunks
    share = rows // n_mem
    me = lax.axis_index("mem")
    i = lax.axis_index("lat")
    x = lax.rem(i, 2)
    y = lax.rem(lax.div(i, 2), 2)
    x_peer = i + 1 - 2 * x
    y_peer = i + 2 - 4 * y
    corner = x == y
    z_target = i + 4 - 8 * x
    z_source = i - 4 + 8 * x
    z_out = corner & (z_target >= 0) & (z_target < n_lat)
    z_in = corner & (z_source >= 0) & (z_source < n_lat)

    def load(m):
        return pltpu.make_async_copy(members_ref.at[m], mem_v.at[m], load_sem.at[m])

    own_rows = pl.ds(pl.multiple_of(me * share, share), share)
    inc_local = pltpu.make_async_copy(inc_ref, inc_v.at[:, own_rows, :], inc_sem)
    inc_local.start()
    for m in range(count):
        load(m).start()

    barrier = pltpu.get_barrier_semaphore()
    for k in range(1, n_mem):
        pl.semaphore_signal(
            barrier, inc=1, device_id={"mem": lax.rem(me + k, n_mem)}, device_id_type=MESH
        )
    pl.semaphore_signal(barrier, inc=1, device_id={"lat": x_peer}, device_id_type=MESH)
    pl.semaphore_signal(barrier, inc=1, device_id={"lat": y_peer}, device_id_type=MESH)

    @pl.when(z_out)
    def _():
        pl.semaphore_signal(barrier, inc=1, device_id={"lat": z_target}, device_id_type=MESH)

    @pl.when(z_in)
    def _():
        pl.semaphore_signal(barrier, inc=1, device_id={"lat": z_source}, device_id_type=MESH)

    pl.semaphore_wait(barrier, n_mem + 1 + z_out.astype(jnp.int32) + z_in.astype(jnp.int32))

    def inc_copy(k):
        return pltpu.make_async_remote_copy(
            src_ref=inc_ref,
            dst_ref=inc_v.at[:, own_rows, :],
            send_sem=inc_send.at[k - 1],
            recv_sem=inc_recv.at[k - 1],
            device_id={"mem": lax.rem(me + k, n_mem)},
            device_id_type=MESH,
        )

    for k in range(1, n_mem):
        inc_copy(k).start()

    def x_copy(k):
        return pltpu.make_async_remote_copy(
            src_ref=own.at[k], dst_ref=buf.at[0, k], send_sem=xs.at[k], recv_sem=xr.at[k],
            device_id={"lat": x_peer}, device_id_type=MESH,
        )

    def y_copy(k):
        return pltpu.make_async_remote_copy(
            src_ref=buf.at[0, k], dst_ref=buf.at[1, k], send_sem=ys.at[k], recv_sem=yr.at[k],
            device_id={"lat": y_peer}, device_id_type=MESH,
        )

    def z_copy(k):
        return pltpu.make_async_remote_copy(
            src_ref=buf.at[1, k], dst_ref=buf.at[2, k], send_sem=zs.at[k], recv_sem=zr.at[k],
            device_id={"lat": z_target}, device_id_type=MESH,
        )

    def part_copy(k, c):
        peer = lax.rem(me + k, n_mem)
        return pltpu.make_async_remote_copy(
            src_ref=acc.at[c, :, pl.ds(pl.multiple_of(peer * share, share), share), :],
            dst_ref=part.at[k - 1, c],
            send_sem=ps.at[k - 1, c],
            recv_sem=pr.at[k - 1, c],
            device_id={"mem": peer},
            device_id_type=MESH,
        )

    contract = (((1,), (1,)), ((), ()))
    spot = lax.broadcasted_iota(jnp.int32, (rows, levels), 0)
    level = lax.broadcasted_iota(jnp.int32, (rows, levels), 1)
    expand = jnp.where(lax.div(spot, slab) == level, 1.0, 0.0)
    tall = jnp.dot(expand, vert_ref[...], precision=HIGHEST, preferred_element_type=jnp.float32)
    gram = lax.dot_general(tall, tall, contract, precision=HIGHEST, preferred_element_type=jnp.float32)
    line = lax.rem(lax.broadcasted_iota(jnp.int32, (rows, LANES), 0), slab)
    lane = lax.broadcasted_iota(jnp.int32, (rows, LANES), 1)
    place = lane + (i * slab - reach)
    inside = (place >= 0) & (place < n_lat * slab)

    def band(offset):
        distance = lane - line - offset
        total = jnp.zeros((rows, LANES), jnp.float32)
        for o in range(taps):
            total = jnp.where(distance == o, lat_ref[o], total)
        return total

    left = jnp.where(inside, band(0), 0.0)
    for slot, offset in ((0, slab * 0), (1, slab * (1 - 2 * x)), (2, slab * (2 * x - 1))):
        block = lax.dot_general(
            left, band(offset), contract, precision=HIGHEST, preferred_element_type=jnp.float32
        )
        mats[slot] = gram * block

    @pl.when(corner & jnp.logical_not(z_in))
    def _():
        @pl.loop(0, items)
        def _(k):
            buf[2, k] = jnp.zeros((rows, LANES), jnp.float32)

    lon_count = lon_ref.shape[0]
    lon_taps = [lon_ref[o] for o in range(lon_count)]
    auto = [
        sum(lon_taps[o] * lon_taps[o + d] for o in range(lon_count - d)) for d in range(lon_count)
    ]

    def piece(m, q):
        at = pl.ds(pl.multiple_of(q * PIECE, PIECE), PIECE)
        total = mem_v[m, 0, at, :].astype(jnp.float32) * inc_v[0, at, :]
        for v in range(1, variables):
            total = total + mem_v[m, v, at, :].astype(jnp.float32) * inc_v[v, at, :]
        smooth = auto[0] * total
        for d in range(1, lon_count):
            smooth = smooth + auto[d] * (
                pltpu.roll(total, d, axis=1) + pltpu.roll(total, lon - d, axis=1)
            )
        for c in range(chunks):
            own[m * chunks + c, at, :] = smooth[:, c * LANES : (c + 1) * LANES]

    def send_member(m):
        @pl.loop(0, chunks)
        def _(c):
            x_copy(m * chunks + c).start()

    per_member = rows // PIECE
    per_step = 2 * per_member // chunks

    inc_local.wait()
    for k in range(1, n_mem):
        inc_copy(k).wait_recv()
    for m in range(count):
        load(m).wait()

    @pl.loop(0, per_member)
    def _(q):
        piece(0, q)

    send_member(0)

    far = 1 + jnp.where(corner, 1, 0)

    def post(k):
        m = lax.div(k, chunks)
        c = lax.rem(k, chunks)
        spread = jnp.dot(mats[0], own[k], precision=HIGHEST, preferred_element_type=jnp.float32)
        spread = spread + jnp.dot(
            mats[1], buf[0, k], precision=HIGHEST, preferred_element_type=jnp.float32
        )
        spread = spread + jnp.dot(
            mats[2], buf[far, k], precision=HIGHEST, preferred_element_type=jnp.float32
        )
        across = pl.ds(pl.multiple_of(c * LANES, LANES), LANES)

        @pl.when(m == 0)
        def _():
            for v in range(variables):
                acc[c, v] = mem_v[m, v, :, across].astype(jnp.float32) * spread

        @pl.when(m > 0)
        def _():
            for v in range(variables):
                acc[c, v] += mem_v[m, v, :, across].astype(jnp.float32) * spread

        @pl.when(m == count - 1)
        def _():
            for j in range(1, n_mem):
                part_copy(j, c).start()

    def step(t, carry):
        @pl.when(t < items)
        def _():
            x_copy(t).wait_recv()
            y_copy(t).start()

        @pl.when((t >= 1) & (t < items + 1))
        def _():
            y_copy(t - 1).wait_recv()

            @pl.when(z_out)
            def _():
                z_copy(t - 1).start()

        first = t * per_step + per_member

        @pl.when(first < count * per_member)
        def _():
            m = lax.div(first, per_member)
            q = lax.rem(first, per_member)

            @pl.loop(0, per_step)
            def _(s):
                piece(m, q + s)

            @pl.when(q + per_step == per_member)
            def _():
                send_member(m)

        @pl.when(t >= 2)
        def _():
            @pl.when(z_in)
            def _():
                z_copy(t - 2).wait_recv()

            post(t - 2)

        return carry

    lax.fori_loop(0, items + 2, step, 0)

    scale = jnp.float32(count * n_mem - 1)

    @pl.loop(0, chunks)
    def _(c):
        for j in range(1, n_mem):
            part_copy(j, c).wait_recv()
        across = pl.ds(pl.multiple_of(c * LANES, LANES), LANES)
        for v in range(variables):
            total = acc[c, v, own_rows, :]
            for j in range(1, n_mem):
                total = total + part[j - 1, c, v]
            out_ref[v, :, across] = total / scale

    @pl.loop(0, items)
    def _(k):
        x_copy(k).wait_send()
        y_copy(k).wait_send()

        @pl.when(z_out)
        def _():
            z_copy(k).wait_send()

    for j in range(1, n_mem):
        inc_copy(j).wait_send()

        @pl.loop(0, chunks)
        def _(c):
            part_copy(j, c).wait_send()


def per_device(n_mem, n_lat, members, increment, vertical, lat_taps, lon_taps):
    count, variables, levels, slab, lon = members.shape
    rows = levels * slab
    share = rows // n_mem
    chunks = lon // LANES
    items = count * chunks
    dma = pltpu.SemaphoreType.DMA
    peers = max(n_mem - 1, 1)
    result = pl.pallas_call(
        functools.partial(kernel, n_mem, n_lat, levels),
        out_shape=jax.ShapeDtypeStruct((variables, share, lon), jnp.float32),
        in_specs=[
            pl.BlockSpec(memory_space=pl.ANY),
            pl.BlockSpec(memory_space=pl.ANY),
            pl.BlockSpec(memory_space=pltpu.VMEM),
            pl.BlockSpec(memory_space=pltpu.SMEM),
            pl.BlockSpec(memory_space=pltpu.SMEM),
        ],
        out_specs=pl.BlockSpec(memory_space=pltpu.VMEM),
        scratch_shapes=[
            pltpu.VMEM((count, variables, rows, lon), jnp.bfloat16),
            pltpu.VMEM((variables, rows, lon), jnp.float32),
            pltpu.VMEM((items, rows, LANES), jnp.float32),
            pltpu.VMEM((3, items, rows, LANES), jnp.float32),
            pltpu.VMEM((chunks, variables, rows, LANES), jnp.float32),
            pltpu.VMEM((peers, chunks, variables, share, LANES), jnp.float32),
            pltpu.VMEM((3, rows, rows), jnp.float32),
            dma((count,)),
            dma,
            dma((peers,)),
            dma((peers,)),
            dma((items,)),
            dma((items,)),
            dma((items,)),
            dma((items,)),
            dma((items,)),
            dma((items,)),
            dma((peers, chunks)),
            dma((peers, chunks)),
        ],
        compiler_params=pltpu.CompilerParams(
            collective_id=0, has_side_effects=True, vmem_limit_bytes=44 * 1024 * 1024
        ),
    )(
        members.reshape(count, variables, rows, lon),
        increment.reshape(variables, share, lon),
        vertical,
        lat_taps,
        lon_taps,
    )
    return result.reshape(increment.shape)


def solution(mesh):
    in_specs = (P("mem", None, None, "lat", None), P(None, "mem", "lat", None), P(), P(), P())
    out_specs = P(None, "mem", "lat", None)
    return jax.shard_map(
        functools.partial(per_device, mesh.shape["mem"], mesh.shape["lat"]),
        mesh=mesh, in_specs=in_specs, out_specs=out_specs, check_vma=False,
    )
```

time: 212 us -> 97.2 us (0.46)
  waiting for transfers between devices: 109 us -> 0 us
  Pallas kernels: 0 us -> 90.1 us
  matrix products: 24.4 us -> 0 us
  local copies, waits for them, and re-layouts: 28.4 us -> 6.39 us
  other arithmetic: 21.9 us -> 0 us
  between operations: 13.8 us -> 0.01 us
  starting transfers between devices: 13.7 us -> 0 us
    pallas_call x0 -> x1, Pallas kernels: none -> 90.1 us  [per_device(): pl.pallas_call(functools.partial(kernel, n_mem, n_lat, levels), out_shape...]
    ppermute x4 -> x0, waiting for transfers between devices: 66.7 us -> none  [the longest x2 40.5 us: extended(): lax.ppermute(lax.slice_in_dim(block, block.shape[dim] - width, None, axis...]
    unnamed x3 -> x0, waiting for transfers between devices: 29.8 us -> none
    dot_general x2 -> x0, matrix products: 24.4 us -> none  [the longest x1 12.5 us: per_device(): jnp.einsum('kl,mkij->mlij', vertical, weighted, precision=lax.Precision.H...]
    add x2 -> x0, other arithmetic: 16.3 us -> none  [the longest x1 8.23 us: lat_forward(): summed = summed + kernel[offset] * padded[..., offset:offset + row_count, :]]
    ppermute x4 -> x0, starting transfers between devices: 13.7 us -> none  [the longest x2 9.35 us: extended(): lax.ppermute(lax.slice_in_dim(block, block.shape[dim] - width, None, axis...]
    all_gather x1 -> x0, waiting for transfers between devices: 12.5 us -> none  [per_device(): increment_all = lax.all_gather(increment, 'mem', axis=1, tiled=True)]
    unnamed x26 -> x11, local copies, waits for them, and re-layouts: 17 us -> 6.39 us
  transfers between devices with their start and end apart: 6 -> 0, of which waited for: 6 -> 0; matrix products, arithmetic and copies ran while one was open for 1% -> 0% of each run, Pallas kernels for 0% -> 0%
where the time goes in v1:
time: 97.2 us; the launch traced here: 96.5 us
  Pallas kernels  90.1 us (93%)
  local copies, waits for them, and re-layouts  6.39 us (7%)
    pallas_call x1, Pallas kernels, per_device(): pl.pallas_call(functools.partial(kernel, n_mem, n_lat, levels), out_shape...  90.1 us
    unnamed x11, local copies, waits for them, and re-layouts  6.39 us

profile of v1, /device:TPU:7, one launch (start us, length us, event | category | flops | bytes accessed | tf_op | source)
XLA Modules:
  0.0 96.5 jit_solution(6077956585649629390)
XLA Ops:
  0.0 0.0 copy-start
  0.0 2.2 %copy-done = bf16[4,4,16,8,1024]{4,3,2,1,0:T(8,128)(2,1)S(1)} copy-done((bf16[4,4,16,8,1024]{4,3,2,1,0:T(8,128)(2,1)S(1)}, bf16[4,4,16,8,1024]{4,3,2,1,0:T(8,128)(2,1)}, u32[]{:S(2)}) %copy-start) | copy-done | bytes 4194328
  2.2 0.0 copy-start.1
  2.2 1.2 %copy-done.1 = f32[4,8,8,1024]{3,2,1,0:T(8,128)S(1)} copy-done((f32[4,8,8,1024]{3,2,1,0:T(8,128)S(1)}, f32[4,8,8,1024]{3,2,1,0:T(8,128)}, u32[]{:S(2)}) %copy-start.1) | copy-done | bytes 1048600
  3.4 0.0 copy-start.2
  3.4 0.7 copy-done.2
  4.1 0.0 copy-start.3
  4.1 0.7 copy-done.3
  4.8 0.0 copy-start.4
  4.8 0.7 copy-done.4
  5.4 90.1 %shard_map.55 = f32[4,64,1024]{2,1,0:T(8,128)S(1)} custom-call(bf16[4,4,128,1024]{3,2,1,0:T(8,128)(2,1)S(1)} %bitcast.3, f32[4,64,1024]{2,1,0:T(8,128)S(1)} %bitcast.5, f32[16,16]{1,0:T(8,128)S(1)} %copy-done.2, f32[9]{0:T(128)S(1)} %copy-done.3, f32[9]{0:T(128)S(1)} %copy-done.4), custom_call_target="tpu_custom_call" | custom-call | tf_op jit(solution)/shard_map/pallas_call | solution.py:287
  95.5 1.0 %copy.7 = f32[4,8,8,1024]{3,2,1,0:T(8,128)} copy(f32[4,8,8,1024]{3,2,1,0:T(8,128)S(1)} %bitcast.4) | data formatting | bytes 2097152
Async XLA Ops:
  0.0 2.2 %copy-start = (bf16[4,4,16,8,1024]{4,3,2,1,0:T(8,128)(2,1)S(1)}, bf16[4,4,16,8,1024]{4,3,2,1,0:T(8,128)(2,1)}, u32[]{:S(2)}) copy-start(bf16[4,4,16,8,1024]{4,3,2,1,0:T(8,128)(2,1)} %param.5) | copy-start | bytes 12582916
  2.2 1.2 %copy-start.1 = (f32[4,8,8,1024]{3,2,1,0:T(8,128)S(1)}, f32[4,8,8,1024]{3,2,1,0:T(8,128)}, u32[]{:S(2)}) copy-start(f32[4,8,8,1024]{3,2,1,0:T(8,128)} %param.6) | copy-start | bytes 3145732
  3.4 0.7 copy-start.2
  4.1 0.7 copy-start.3
  4.8 0.7 copy-start.4

commit v2 on v1

--- a/solution.py
+++ b/solution.py
@@ -8,13 +8,17 @@
 from jax.sharding import PartitionSpec as P
 
 LANES = 128
+Y_LAG = 3
+Z_LAG = 6
+AHEAD = 4
 PIECE = 16
 HIGHEST = lax.Precision.HIGHEST
 MESH = pl.DeviceIdType.MESH
 
 
 def kernel(
-    n_mem, n_lat, levels, members_ref, inc_ref, vert_ref, lat_ref, lon_ref, out_ref,
+    n_mem, n_lat, levels, members_ref, inc_ref, vert_hbm, lat_hbm, lon_hbm, out_ref,
+    vert_ref, lat_ref, lon_ref, small_sem,
     mem_v, inc_v, own, buf, acc, part, mats,
     load_sem, inc_sem, inc_send, inc_recv, xs, xr, ys, yr, zs, zr, ps, pr,
 ):
@@ -46,6 +50,15 @@
     for m in range(count):
         load(m).start()
 
+    small = [
+        pltpu.make_async_copy(source, target, small_sem.at[n])
+        for n, (source, target) in enumerate(
+            ((vert_hbm, vert_ref), (lat_hbm, lat_ref), (lon_hbm, lon_ref))
+        )
+    ]
+    for copy in small:
+        copy.start()
+
     barrier = pltpu.get_barrier_semaphore()
     for k in range(1, n_mem):
         pl.semaphore_signal(
@@ -105,6 +118,9 @@
             device_id={"mem": peer},
             device_id_type=MESH,
         )
+
+    for copy in small:
+        copy.wait()
 
     contract = (((1,), (1,)), ((), ()))
     spot = lax.broadcasted_iota(jnp.int32, (rows, levels), 0)
@@ -156,11 +172,6 @@
         for c in range(chunks):
             own[m * chunks + c, at, :] = smooth[:, c * LANES : (c + 1) * LANES]
 
-    def send_member(m):
-        @pl.loop(0, chunks)
-        def _(c):
-            x_copy(m * chunks + c).start()
-
     per_member = rows // PIECE
     per_step = 2 * per_member // chunks
 
@@ -174,7 +185,9 @@
     def _(q):
         piece(0, q)
 
-    send_member(0)
+    @pl.loop(0, AHEAD)
+    def _(k):
+        x_copy(k).start()
 
     far = 1 + jnp.where(corner, 1, 0)
 
@@ -211,13 +224,17 @@
             x_copy(t).wait_recv()
             y_copy(t).start()
 
-        @pl.when((t >= 1) & (t < items + 1))
-        def _():
-            y_copy(t - 1).wait_recv()
+        @pl.when(t + AHEAD < items)
+        def _():
+            x_copy(t + AHEAD).start()
+
+        @pl.when((t >= Y_LAG) & (t < items + Y_LAG))
+        def _():
+            y_copy(t - Y_LAG).wait_recv()
 
             @pl.when(z_out)
             def _():
-                z_copy(t - 1).start()
+                z_copy(t - Y_LAG).start()
 
         first = t * per_step + per_member
 
@@ -230,21 +247,17 @@
             def _(s):
                 piece(m, q + s)
 
-            @pl.when(q + per_step == per_member)
-            def _():
-                send_member(m)
-
-        @pl.when(t >= 2)
+        @pl.when(t >= Z_LAG)
         def _():
             @pl.when(z_in)
             def _():
-                z_copy(t - 2).wait_recv()
-
-            post(t - 2)
+                z_copy(t - Z_LAG).wait_recv()
+
+            post(t - Z_LAG)
 
         return carry
 
-    lax.fori_loop(0, items + 2, step, 0)
+    lax.fori_loop(0, items + Z_LAG, step, 0)
 
     scale = jnp.float32(count * n_mem - 1)
 
@@ -288,14 +301,18 @@
         functools.partial(kernel, n_mem, n_lat, levels),
         out_shape=jax.ShapeDtypeStruct((variables, share, lon), jnp.float32),
         in_specs=[
-            pl.BlockSpec(memory_space=pl.ANY),
-            pl.BlockSpec(memory_space=pl.ANY),
-            pl.BlockSpec(memory_space=pltpu.VMEM),
-            pl.BlockSpec(memory_space=pltpu.SMEM),
-            pl.BlockSpec(memory_space=pltpu.SMEM),
+            pl.BlockSpec(memory_space=pltpu.HBM),
+            pl.BlockSpec(memory_space=pltpu.HBM),
+            pl.BlockSpec(memory_space=pltpu.HBM),
+            pl.BlockSpec(memory_space=pltpu.HBM),
+            pl.BlockSpec(memory_space=pltpu.HBM),
         ],
         out_specs=pl.BlockSpec(memory_space=pltpu.VMEM),
         scratch_shapes=[
+            pltpu.VMEM(vertical.shape, jnp.float32),
+            pltpu.SMEM(lat_taps.shape, jnp.float32),
+            pltpu.SMEM(lon_taps.shape, jnp.float32),
+            dma((3,)),
             pltpu.VMEM((count, variables, rows, lon), jnp.bfloat16),
             pltpu.VMEM((variables, rows, lon), jnp.float32),
             pltpu.VMEM((items, rows, LANES), jnp.float32),
@@ -317,7 +334,7 @@
             dma((peers, chunks)),
         ],
         compiler_params=pltpu.CompilerParams(
-            collective_id=0, has_side_effects=True, vmem_limit_bytes=44 * 1024 * 1024
+            collective_id=0, has_side_effects=True, vmem_limit_bytes=60 * 1024 * 1024
         ),
     )(
         members.reshape(count, variables, rows, lon),

time: 97.2 us -> 69.3 us (0.71)
  Pallas kernels: 90.1 us -> 66.9 us
  local copies, waits for them, and re-layouts: 6.39 us -> 2.31 us
    pallas_call x1, Pallas kernels: 90.1 us -> 66.9 us  [per_device(): pl.pallas_call(functools.partial(kernel, n_mem, n_lat, levels), out_shape...]
    unnamed x11 -> x1, local copies, waits for them, and re-layouts: 6.39 us -> 2.31 us
where the time goes in v2:
time: 69.3 us; the launch traced here: 69.2 us
  Pallas kernels  66.9 us (97%)
  local copies, waits for them, and re-layouts  2.31 us (3%)
    pallas_call x1, Pallas kernels, per_device(): pl.pallas_call(functools.partial(kernel, n_mem, n_lat, levels), out_shape...  66.9 us
    unnamed x1, local copies, waits for them, and re-layouts  2.31 us

profile of v2, /device:TPU:7, one launch (start us, length us, event | category | flops | bytes accessed | tf_op | source)
XLA Modules:
  0.0 69.2 jit_solution(15507325690376298412)
XLA Ops:
  0.0 66.9 %shard_map.55 = f32[4,64,1024]{2,1,0:T(8,128)} custom-call(bf16[4,4,128,1024]{3,2,1,0:T(8,128)(2,1)} %bitcast.3, f32[4,64,1024]{2,1,0:T(8,128)} %bitcast.5, f32[16,16]{1,0:T(8,128)} %vert_hbm.1, f32[9]{0:T(128)} %lat_hbm.1, f32[9]{0:T(128)} %lon_hbm.1), custom_call_target="tpu_custom_call" | custom-call | tf_op jit(solution)/shard_map/pallas_call | solution.py:300
  66.9 2.3 %copy.7 = f32[4,8,8,1024]{3,2,1,0:T(8,128)} copy(f32[4,8,8,1024]{3,2,1,0:T(8,128)} %bitcast.4) | data formatting | bytes 2097152

commit v3 on v2

--- a/solution.py
+++ b/solution.py
@@ -11,7 +11,6 @@
 Y_LAG = 3
 Z_LAG = 6
 AHEAD = 4
-PIECE = 16
 HIGHEST = lax.Precision.HIGHEST
 MESH = pl.DeviceIdType.MESH
 
@@ -28,6 +27,7 @@
     reach = taps // 2
     chunks = lon // LANES
     items = count * chunks
+    width = rows // chunks
     share = rows // n_mem
     me = lax.axis_index("mem")
     i = lax.axis_index("lat")
@@ -90,21 +90,33 @@
     for k in range(1, n_mem):
         inc_copy(k).start()
 
-    def x_copy(k):
-        return pltpu.make_async_remote_copy(
-            src_ref=own.at[k], dst_ref=buf.at[0, k], send_sem=xs.at[k], recv_sem=xr.at[k],
+    def own_item(k, early):
+        return own.at[:chunks, pl.ds(pl.multiple_of(k * width, width), width), :] if early else own.at[k]
+
+    def item(n, k, early):
+        if early:
+            return buf.at[n, :chunks, pl.ds(pl.multiple_of(k * width, width), width), :]
+        return buf.at[n, k]
+
+    def each(k, act):
+        pl.when(k < chunks)(lambda: act(k, True))
+        pl.when(k >= chunks)(lambda: act(k, False))
+
+    def x_copy(k, early):
+        return pltpu.make_async_remote_copy(
+            src_ref=own_item(k, early), dst_ref=item(0, k, early), send_sem=xs.at[k], recv_sem=xr.at[k],
             device_id={"lat": x_peer}, device_id_type=MESH,
         )
 
-    def y_copy(k):
-        return pltpu.make_async_remote_copy(
-            src_ref=buf.at[0, k], dst_ref=buf.at[1, k], send_sem=ys.at[k], recv_sem=yr.at[k],
+    def y_copy(k, early):
+        return pltpu.make_async_remote_copy(
+            src_ref=item(0, k, early), dst_ref=item(1, k, early), send_sem=ys.at[k], recv_sem=yr.at[k],
             device_id={"lat": y_peer}, device_id_type=MESH,
         )
 
-    def z_copy(k):
-        return pltpu.make_async_remote_copy(
-            src_ref=buf.at[1, k], dst_ref=buf.at[2, k], send_sem=zs.at[k], recv_sem=zr.at[k],
+    def z_copy(k, early):
+        return pltpu.make_async_remote_copy(
+            src_ref=item(1, k, early), dst_ref=item(2, k, early), send_sem=zs.at[k], recv_sem=zr.at[k],
             device_id={"lat": z_target}, device_id_type=MESH,
         )
 
@@ -160,7 +172,7 @@
     ]
 
     def piece(m, q):
-        at = pl.ds(pl.multiple_of(q * PIECE, PIECE), PIECE)
+        at = pl.ds(pl.multiple_of(q * width, width), width)
         total = mem_v[m, 0, at, :].astype(jnp.float32) * inc_v[0, at, :]
         for v in range(1, variables):
             total = total + mem_v[m, v, at, :].astype(jnp.float32) * inc_v[v, at, :]
@@ -172,22 +184,17 @@
         for c in range(chunks):
             own[m * chunks + c, at, :] = smooth[:, c * LANES : (c + 1) * LANES]
 
-    per_member = rows // PIECE
-    per_step = 2 * per_member // chunks
+    per_step = 2
 
     inc_local.wait()
     for k in range(1, n_mem):
         inc_copy(k).wait_recv()
-    for m in range(count):
-        load(m).wait()
-
-    @pl.loop(0, per_member)
+    load(0).wait()
+
+    @pl.loop(0, chunks)
     def _(q):
         piece(0, q)
-
-    @pl.loop(0, AHEAD)
-    def _(k):
-        x_copy(k).start()
+        x_copy(q, True).start()
 
     far = 1 + jnp.where(corner, 1, 0)
 
@@ -221,27 +228,37 @@
     def step(t, carry):
         @pl.when(t < items)
         def _():
-            x_copy(t).wait_recv()
-            y_copy(t).start()
-
-        @pl.when(t + AHEAD < items)
-        def _():
-            x_copy(t + AHEAD).start()
+            def act(k, early):
+                x_copy(k, early).wait_recv()
+                y_copy(k, early).start()
+
+            each(t, act)
+
+        @pl.when((t + AHEAD >= chunks) & (t + AHEAD < items))
+        def _():
+            x_copy(t + AHEAD, False).start()
 
         @pl.when((t >= Y_LAG) & (t < items + Y_LAG))
         def _():
-            y_copy(t - Y_LAG).wait_recv()
-
-            @pl.when(z_out)
+            def act(k, early):
+                y_copy(k, early).wait_recv()
+
+                @pl.when(z_out)
+                def _():
+                    z_copy(k, early).start()
+
+            each(t - Y_LAG, act)
+
+        first = t * per_step + chunks
+
+        @pl.when(first < count * chunks)
+        def _():
+            m = lax.div(first, chunks)
+            q = lax.rem(first, chunks)
+
+            @pl.when(q == 0)
             def _():
-                z_copy(t - Y_LAG).start()
-
-        first = t * per_step + per_member
-
-        @pl.when(first < count * per_member)
-        def _():
-            m = lax.div(first, per_member)
-            q = lax.rem(first, per_member)
+                load(m).wait()
 
             @pl.loop(0, per_step)
             def _(s):
@@ -251,8 +268,18 @@
         def _():
             @pl.when(z_in)
             def _():
-                z_copy(t - Z_LAG).wait_recv()
-
+                each(t - Z_LAG, lambda k, early: z_copy(k, early).wait_recv())
+
+        begin = chunks - 1 + Z_LAG
+
+        @pl.when((t >= begin) & (t < begin + chunks - 1))
+        def _():
+            @pl.loop(0, 2)
+            def _(s):
+                post(2 * (t - begin) + s)
+
+        @pl.when(t >= begin + chunks - 1)
+        def _():
             post(t - Z_LAG)
 
         return carry
@@ -274,12 +301,15 @@
 
     @pl.loop(0, items)
     def _(k):
-        x_copy(k).wait_send()
-        y_copy(k).wait_send()
-
-        @pl.when(z_out)
-        def _():
-            z_copy(k).wait_send()
+        def act(k, early):
+            x_copy(k, early).wait_send()
+            y_copy(k, early).wait_send()
+
+            @pl.when(z_out)
+            def _():
+                z_copy(k, early).wait_send()
+
+        each(k, act)
 
     for j in range(1, n_mem):
         inc_copy(j).wait_send()

time: 69.3 us -> 67 us (0.967)
  Pallas kernels: 66.9 us -> 64.5 us
    pallas_call x1, Pallas kernels: 66.9 us -> 64.5 us  [per_device(): pl.pallas_call(functools.partial(kernel, n_mem, n_lat, levels), out_shape...]
where the time goes in v3:
time: 67 us; the launch traced here: 66.8 us
  Pallas kernels  64.5 us (96%)
  local copies, waits for them, and re-layouts  2.31 us (3%)
    pallas_call x1, Pallas kernels, per_device(): pl.pallas_call(functools.partial(kernel, n_mem, n_lat, levels), out_shape...  64.5 us
    unnamed x1, local copies, waits for them, and re-layouts  2.31 us

profile of v3, /device:TPU:7, one launch (start us, length us, event | category | flops | bytes accessed | tf_op | source)
XLA Modules:
  0.0 66.8 jit_solution(13335550600470927137)
XLA Ops:
  0.0 64.5 %shard_map.55 = f32[4,64,1024]{2,1,0:T(8,128)} custom-call(bf16[4,4,128,1024]{3,2,1,0:T(8,128)(2,1)} %bitcast.3, f32[4,64,1024]{2,1,0:T(8,128)} %bitcast.5, f32[16,16]{1,0:T(8,128)} %vert_hbm.1, f32[9]{0:T(128)} %lat_hbm.1, f32[9]{0:T(128)} %lon_hbm.1), custom_call_target="tpu_custom_call" | custom-call | tf_op jit(solution)/shard_map/pallas_call | solution.py:330
  64.5 2.3 %copy.7 = f32[4,8,8,1024]{3,2,1,0:T(8,128)} copy(f32[4,8,8,1024]{3,2,1,0:T(8,128)} %bitcast.4) | data formatting | bytes 2097152

commit v4 on v3

--- a/solution.py
+++ b/solution.py
@@ -29,6 +29,7 @@
     items = count * chunks
     width = rows // chunks
     share = rows // n_mem
+    own_bands = share // width if share % width == 0 else 0
     me = lax.axis_index("mem")
     i = lax.axis_index("lat")
     x = lax.rem(i, 2)
@@ -90,12 +91,16 @@
     for k in range(1, n_mem):
         inc_copy(k).start()
 
+    def band_rows(k):
+        turn = lax.rem(me * own_bands + k, chunks)
+        return pl.ds(pl.multiple_of(turn * width, width), width)
+
     def own_item(k, early):
-        return own.at[:chunks, pl.ds(pl.multiple_of(k * width, width), width), :] if early else own.at[k]
+        return own.at[:chunks, band_rows(k), :] if early else own.at[k]
 
     def item(n, k, early):
         if early:
-            return buf.at[n, :chunks, pl.ds(pl.multiple_of(k * width, width), width), :]
+            return buf.at[n, :chunks, band_rows(k), :]
         return buf.at[n, k]
 
     def each(k, act):
@@ -133,37 +138,6 @@
 
     for copy in small:
         copy.wait()
-
-    contract = (((1,), (1,)), ((), ()))
-    spot = lax.broadcasted_iota(jnp.int32, (rows, levels), 0)
-    level = lax.broadcasted_iota(jnp.int32, (rows, levels), 1)
-    expand = jnp.where(lax.div(spot, slab) == level, 1.0, 0.0)
-    tall = jnp.dot(expand, vert_ref[...], precision=HIGHEST, preferred_element_type=jnp.float32)
-    gram = lax.dot_general(tall, tall, contract, precision=HIGHEST, preferred_element_type=jnp.float32)
-    line = lax.rem(lax.broadcasted_iota(jnp.int32, (rows, LANES), 0), slab)
-    lane = lax.broadcasted_iota(jnp.int32, (rows, LANES), 1)
-    place = lane + (i * slab - reach)
-    inside = (place >= 0) & (place < n_lat * slab)
-
-    def band(offset):
-        distance = lane - line - offset
-        total = jnp.zeros((rows, LANES), jnp.float32)
-        for o in range(taps):
-            total = jnp.where(distance == o, lat_ref[o], total)
-        return total
-
-    left = jnp.where(inside, band(0), 0.0)
-    for slot, offset in ((0, slab * 0), (1, slab * (1 - 2 * x)), (2, slab * (2 * x - 1))):
-        block = lax.dot_general(
-            left, band(offset), contract, precision=HIGHEST, preferred_element_type=jnp.float32
-        )
-        mats[slot] = gram * block
-
-    @pl.when(corner & jnp.logical_not(z_in))
-    def _():
-        @pl.loop(0, items)
-        def _(k):
-            buf[2, k] = jnp.zeros((rows, LANES), jnp.float32)
 
     lon_count = lon_ref.shape[0]
     lon_taps = [lon_ref[o] for o in range(lon_count)]
@@ -186,15 +160,48 @@
 
     per_step = 2
 
+    def first_band(k):
+        piece(0, lax.rem(me * own_bands + k, chunks))
+        x_copy(k, True).start()
+
     inc_local.wait()
+    load(0).wait()
+    pl.loop(0, own_bands)(first_band)
+
+    contract = (((1,), (1,)), ((), ()))
+    spot = lax.broadcasted_iota(jnp.int32, (rows, levels), 0)
+    level = lax.broadcasted_iota(jnp.int32, (rows, levels), 1)
+    expand = jnp.where(lax.div(spot, slab) == level, 1.0, 0.0)
+    tall = jnp.dot(expand, vert_ref[...], precision=HIGHEST, preferred_element_type=jnp.float32)
+    gram = lax.dot_general(tall, tall, contract, precision=HIGHEST, preferred_element_type=jnp.float32)
+    line = lax.rem(lax.broadcasted_iota(jnp.int32, (rows, LANES), 0), slab)
+    lane = lax.broadcasted_iota(jnp.int32, (rows, LANES), 1)
+    place = lane + (i * slab - reach)
+    inside = (place >= 0) & (place < n_lat * slab)
+
+    def band(offset):
+        distance = lane - line - offset
+        total = jnp.zeros((rows, LANES), jnp.float32)
+        for o in range(taps):
+            total = jnp.where(distance == o, lat_ref[o], total)
+        return total
+
+    left = jnp.where(inside, band(0), 0.0)
+    for slot, offset in ((0, slab * 0), (1, slab * (1 - 2 * x)), (2, slab * (2 * x - 1))):
+        block = lax.dot_general(
+            left, band(offset), contract, precision=HIGHEST, preferred_element_type=jnp.float32
+        )
+        mats[slot] = gram * block
+
+    @pl.when(corner & jnp.logical_not(z_in))
+    def _():
+        @pl.loop(0, items)
+        def _(k):
+            buf[2, k] = jnp.zeros((rows, LANES), jnp.float32)
+
     for k in range(1, n_mem):
         inc_copy(k).wait_recv()
-    load(0).wait()
-
-    @pl.loop(0, chunks)
-    def _(q):
-        piece(0, q)
-        x_copy(q, True).start()
+    pl.loop(own_bands, chunks)(first_band)
 
     far = 1 + jnp.where(corner, 1, 0)
 

time: 67 us -> 64.9 us (0.969)
  Pallas kernels: 64.5 us -> 62.5 us
    pallas_call x1, Pallas kernels: 64.5 us -> 62.5 us  [per_device(): pl.pallas_call(functools.partial(kernel, n_mem, n_lat, levels), out_shape...]
where the time goes in v4:
time: 64.9 us; the launch traced here: 64.8 us
  Pallas kernels  62.5 us (96%)
  local copies, waits for them, and re-layouts  2.31 us (4%)
    pallas_call x1, Pallas kernels, per_device(): pl.pallas_call(functools.partial(kernel, n_mem, n_lat, levels), out_shape...  62.5 us
    unnamed x1, local copies, waits for them, and re-layouts  2.31 us

profile of v4, /device:TPU:7, one launch (start us, length us, event | category | flops | bytes accessed | tf_op | source)
XLA Modules:
  0.0 64.8 jit_solution(13182508943059537962)
XLA Ops:
  0.0 62.5 %shard_map.55 = f32[4,64,1024]{2,1,0:T(8,128)} custom-call(bf16[4,4,128,1024]{3,2,1,0:T(8,128)(2,1)} %bitcast.3, f32[4,64,1024]{2,1,0:T(8,128)} %bitcast.5, f32[16,16]{1,0:T(8,128)} %vert_hbm.1, f32[9]{0:T(128)} %lat_hbm.1, f32[9]{0:T(128)} %lon_hbm.1), custom_call_target="tpu_custom_call" | custom-call | tf_op jit(solution)/shard_map/pallas_call | solution.py:337
  62.5 2.3 %copy.7 = f32[4,8,8,1024]{3,2,1,0:T(8,128)} copy(f32[4,8,8,1024]{3,2,1,0:T(8,128)} %bitcast.4) | data formatting | bytes 2097152

commit v5 on v4

--- a/solution.py
+++ b/solution.py
@@ -293,6 +293,18 @@
 
     lax.fori_loop(0, items + Z_LAG, step, 0)
 
+    @pl.loop(0, items)
+    def _(k):
+        def act(k, early):
+            x_copy(k, early).wait_send()
+            y_copy(k, early).wait_send()
+
+            @pl.when(z_out)
+            def _():
+                z_copy(k, early).wait_send()
+
+        each(k, act)
+
     scale = jnp.float32(count * n_mem - 1)
 
     @pl.loop(0, chunks)
@@ -305,18 +317,6 @@
             for j in range(1, n_mem):
                 total = total + part[j - 1, c, v]
             out_ref[v, :, across] = total / scale
-
-    @pl.loop(0, items)
-    def _(k):
-        def act(k, early):
-            x_copy(k, early).wait_send()
-            y_copy(k, early).wait_send()
-
-            @pl.when(z_out)
-            def _():
-                z_copy(k, early).wait_send()
-
-        each(k, act)
 
     for j in range(1, n_mem):
         inc_copy(j).wait_send()

time: 64.9 us -> 64.5 us (level)
  no operation moved by 1% of the time
where the time goes in v5:
time: 64.5 us; the launch traced here: 64.4 us
  Pallas kernels  62.1 us (96%)
  local copies, waits for them, and re-layouts  2.31 us (4%)
    pallas_call x1, Pallas kernels, per_device(): pl.pallas_call(functools.partial(kernel, n_mem, n_lat, levels), out_shape...  62.1 us
    unnamed x1, local copies, waits for them, and re-layouts  2.31 us

profile of v5, /device:TPU:7, one launch (start us, length us, event | category | flops | bytes accessed | tf_op | source)
XLA Modules:
  0.0 64.4 jit_solution(10262034510470627256)
XLA Ops:
  0.0 62.1 %shard_map.55 = f32[4,64,1024]{2,1,0:T(8,128)} custom-call(bf16[4,4,128,1024]{3,2,1,0:T(8,128)(2,1)} %bitcast.3, f32[4,64,1024]{2,1,0:T(8,128)} %bitcast.5, f32[16,16]{1,0:T(8,128)} %vert_hbm.1, f32[9]{0:T(128)} %lat_hbm.1, f32[9]{0:T(128)} %lon_hbm.1), custom_call_target="tpu_custom_call" | custom-call | tf_op jit(solution)/shard_map/pallas_call | solution.py:337
  62.1 2.3 %copy.7 = f32[4,8,8,1024]{3,2,1,0:T(8,128)} copy(f32[4,8,8,1024]{3,2,1,0:T(8,128)} %bitcast.4) | data formatting | bytes 2097152
